TPU v7x, 32 devices: a whole 2x2x4 slice. The times are simulated.
32 devices in a mesh: dp: 4 (over y, x), space: 8 (over z, core).
Axes of the slice: x: 2, y: 2, z: 4, core: 2. Of those that a mesh axis runs over, the one named last changes fastest.
Arguments:
- volume: bfloat16 [4, 128, 16, 16, 256], P('dp', None, 'space'), may hold values from -6 to 6
- w_first: bfloat16 [3, 3, 3, 128, 256], replicated, may hold values from -0.109375 to 0.109375
- w_second: bfloat16 [3, 3, 3, 256, 512], P(None, None, None, 'space'), may hold values from -0.078125 to 0.078125
- cotangent: bfloat16 [4, 512, 4, 256], P('dp', 'space'), may hold values from -6 to 6
Outputs:
- grad_second: float32 [3, 3, 3, 256, 512], P(None, None, None, 'space')
- pre_grad: bfloat16 [4, 256, 8, 4, 256], P('dp', None, 'space')
All inputs are finite; a program needn't handle non-finite values.
Results may differ from a plain program's by a relative error of at most 0.0049.
Values may be sent and summed in bfloat16 or wider, within the bound.
A program may use at most 128 MiB of HBM per device.

v0:
```python
import jax
import jax.numpy as jnp
from jax import lax
from jax.sharding import PartitionSpec as P

C3 = 512
WID = 128


leak_slope = 0.3


def from_behind(block, axis, distance):
    devices = range(lax.axis_size(axis))
    route = [(i - distance, i) for i in devices if i - distance in devices]
    return lax.ppermute(block, axis, route)


def activate(values):
    return leak_slope * values + (1.0 - leak_slope) * values * jax.nn.sigmoid(values)


def slope_of(values):
    sigmoid_value = jax.nn.sigmoid(values)
    return leak_slope + (1.0 - leak_slope) * (
        sigmoid_value + values * sigmoid_value * (1.0 - sigmoid_value)
    )


def stride_taps(values, along_dim):
    length = values.shape[along_dim] // 2
    paired = values.reshape(values.shape[:along_dim] + (length, 2) + values.shape[along_dim + 1 :])
    even_cells = lax.index_in_dim(paired, 0, along_dim + 1, keepdims=False)
    odd_cells = lax.index_in_dim(paired, 1, along_dim + 1, keepdims=False)
    before = jnp.concatenate(
        [
            jnp.zeros_like(lax.slice_in_dim(odd_cells, 0, 1, axis=along_dim)),
            lax.slice_in_dim(odd_cells, 0, length - 1, axis=along_dim),
        ],
        along_dim,
    )
    return [before, even_cells, odd_cells]


def step_cells(values, by_row, by_col, row_len):
    cells = values.shape[-1]
    if by_row:
        filler = jnp.zeros(values.shape[:-1] + (row_len,), values.dtype)
        values = jnp.concatenate([filler, values[..., : cells - row_len]], -1)
    if by_col:
        filler = jnp.zeros(values.shape[:-1] + (1,), values.dtype)
        moved = jnp.concatenate([filler, values[..., : cells - 1]], -1)
        keeper = lax.iota(jnp.int32, cells) % row_len != 0
        values = jnp.where(keeper, moved, jnp.zeros_like(moved))
    return values


def plane_taps(values, row_len):
    phases = values.shape[-2]
    out_phases = phases // 2
    collected = []
    for row_tap in range(3):
        for col_tap in range(3):
            rows_out = []
            for row_phase in range(out_phases):
                cols_out = []
                for col_phase in range(out_phases):
                    row_at = 2 * row_phase + row_tap - 1
                    col_at = 2 * col_phase + col_tap - 1
                    part = values[..., row_at % phases, col_at % phases, :]
                    cols_out.append(step_cells(part, row_at < 0, col_at < 0, row_len))
                rows_out.append(jnp.stack(cols_out, -2))
            collected.append(jnp.stack(rows_out, -3))
    return collected


def all_taps(values, row_len):
    collected = []
    for depth_part in stride_taps(values, 1):
        collected.extend(plane_taps(depth_part, row_len))
    return collected


def contract_first(left_side, right_side):
    return lax.dot_general(
        left_side, right_side, (((0,), (0,)), ((), ())), preferred_element_type=jnp.float32
    )


def contract_last(left_side, right_side):
    return lax.dot_general(
        left_side, right_side, (((1,), (1,)), ((), ())), preferred_element_type=jnp.float32
    )


def per_device(volume, w_first, w_second, cotangent):
    channels = volume.shape[1]
    depth_cells = volume.shape[2]
    cell_count = volume.shape[4]
    half_depth = depth_cells // 2
    out_channels = w_first.shape[4]
    row_len = WID // 4
    paired = volume[0].reshape(channels, half_depth, 2, 4, 4, cell_count)
    even_cells = paired[:, :, 0]
    odd_cells = paired[:, :, 1]
    w_flat = w_first.reshape(27 * channels, out_channels)
    rim_cells = from_behind(odd_cells, "space", 1)
    before = jnp.concatenate([rim_cells, odd_cells[:, : half_depth - 1]], 1)
    collected = []
    for depth_part in (before, even_cells, odd_cells):
        collected.extend(plane_taps(depth_part, row_len))
    stacked = jnp.stack(collected, 0).reshape(27 * channels, -1)
    pre_act = contract_first(w_flat, stacked).reshape(out_channels, half_depth, 4, cell_count)
    hidden = activate(pre_act).astype(jnp.bfloat16)
    by_channel = lax.all_to_all(hidden, "space", split_axis=0, concat_axis=1, tiled=True)
    own_channels = by_channel.shape[0]
    full_depth = by_channel.shape[1]
    hidden_cells = by_channel.reshape(own_channels, full_depth, 2, 2, cell_count)
    hidden_taps = jnp.stack(all_taps(hidden_cells, row_len), 0).reshape(27 * own_channels, -1)
    w_rows = w_second.reshape(27 * own_channels, C3)
    out_cells = hidden_taps.shape[1]
    gathered = lax.all_gather(cotangent[0], "space", axis=0, tiled=True)
    cot_flat = gathered.reshape(C3, out_cells)
    weight_grad = contract_last(hidden_taps, cot_flat)
    tap_terms = jnp.dot(w_rows, cot_flat, preferred_element_type=jnp.float32)
    grad_second = lax.psum(weight_grad, "dp").reshape(3, 3, 3, own_channels, C3)

    def spread(field):
        return jnp.stack(all_taps(field, row_len), 0).reshape(27 * own_channels, -1)

    unused, pull = jax.vjp(
        spread, jnp.zeros((own_channels, full_depth, 2, 2, cell_count), jnp.float32)
    )
    back_terms = pull(tap_terms)[0]
    back_terms = back_terms.astype(jnp.bfloat16).reshape(own_channels, full_depth, 4, cell_count)
    hidden_grad = lax.all_to_all(back_terms, "space", split_axis=1, concat_axis=0, tiled=True)
    pre_grad = (hidden_grad.astype(jnp.float32) * slope_of(pre_act)).astype(jnp.bfloat16)
    return (grad_second, pre_grad[None])


def solution(mesh):
    in_specs = (
        P("dp", None, "space", None, None),
        P(),
        P(None, None, None, "space", None),
        P("dp", "space", None, None),
    )
    out_specs = (P(None, None, None, "space", None), P("dp", None, "space", None, None))
    return jax.shard_map(
        per_device, mesh=mesh, in_specs=in_specs, out_specs=out_specs, check_vma=False
    )
```

profile of v0, /device:TPU:0, one launch (start us, length us, event | category | flops | bytes accessed | tf_op | source)
XLA Modules:
  0.0 226.3 jit_solution(15564648068313513409)
XLA Ops:
  7.2 2.9 %copy.103 = bf16[1,128,2,16,256]{4,1,3,2,0:T(8,128)(2,1)S(1)} copy(bf16[1,128,2,16,256]{4,3,2,1,0:T(8,128)(2,1)} %param.4) | data formatting | bytes 4194304 | tf_op args[0]
  10.1 1.1 slice_bitcast_fusion
  11.2 3.4 %collective-permute-start = (bf16[128,1,4,4,256]{4,0,3,2,1:T(8,128)(2,1)S(1)}, bf16[128,1,4,4,256]{4,0,3,2,1:T(8,128)(2,1)}, u32[]{:S(2)}, u32[]{:S(2)}) collective-permute-start(bf16[128,1,4,4,256]{4,0,3,2,1:T(8,128)(2,1)S(1)} %get-tuple-element.34), channel_id=1, source_target_pairs={{0,1},{1,2},{2,3},{3,4},{4,5},{5,6},{6,7},{8,9},{9,10},{10,11},{11... | collective-permute-start | bytes 3145736 | tf_op jit(solution)/shard_map/ppermute | solution.py:16
  15.6 1.4 slice_bitcast_fusion.65
  19.3 1.4 slice_bitcast_fusion.79
  22.6 6.8 %copy.104 = bf16[27,128,1,2,2,256]{5,4,3,1,0,2:T(2,128)(2,1)} copy(bf16[27,128,1,2,2,256]{5,1,4,3,2,0:T(8,128)(2,1)S(1)} %fusion.33) | data formatting | bytes 14155776 | tf_op jit(solution)/shard_map/stack | solution.py:112
  29.4 16.2 %reshape.233 = bf16[3456,1024]{1,0:T(8,128)(2,1)} reshape(bf16[27,128,1,2,2,256]{5,4,3,1,0,2:T(2,128)(2,1)} %copy.104) | data formatting | bytes 14155776 | tf_op jit(solution)/shard_map/reshape | solution.py:112
  45.6 6.2 %fusion.2 = (bf16[256,1024]{0,1:T(8,128)(2,1)S(1)}, f32[1024,256]{1,0:T(8,128)}) fusion(bf16[3456,1024]{1,0:T(8,128)(2,1)} %reshape.233, bf16[3456,256]{1,0:T(8,128)(2,1)S(1)} %bitcast.635), kind=kOutput, calls=%fused_computation.9 | convolution fusion | flops 1814036480 | bytes 10420224 | tf_op jit(solution)/shard_map/dot_general | solution.py:85
  51.8 1.1 copy.105
  52.8 24.1 %all-to-all-start = ((bf16[256,1,4,256]{3,2,1,0:T(4,128)(2,1)}), bf16[256,1,4,256]{3,2,1,0:T(4,128)(2,1)S(1)}, u32[]{:S(2)}, u32[]{:S(2)}) async-start(bf16[256,1,4,256]{3,2,1,0:T(4,128)(2,1)} %copy.105), calls=%async_computation | async-start | bytes 1048576 | tf_op jit(solution)/shard_map/all_to_all | solution.py:115
  77.2 1.4 copy.175
  78.7 1.1 fusion.42
  80.5 1.1 fusion.39
  81.6 1.6 unstack.167
  83.2 1.7 split.76
  84.9 1.6 unstack.197
  86.5 1.7 split.85
  88.2 1.6 unstack.173
  89.8 1.7 split.77
  91.5 1.6 unstack.179
  93.1 1.7 split.80
  94.8 1.6 unstack.185
  96.4 1.7 split.81
  98.1 1.6 unstack.203
  99.7 1.7 split.87
  101.4 1.6 unstack.209
  103.0 1.7 split.88
  104.7 1.6 unstack.215
  106.3 1.7 split.91
  108.7 1.0 split.82
  109.8 2.4 %copy_select_fusion.6 = (f32[32,4,255]{2,0,1:T(8,128)}, f32[32,4,255]{2,0,1:T(8,128)S(1)}, f32[32,4,255]{2,0,1:T(8,128)}, f32[32,4,255]{2,0,1:T(8,128)S(1)}, f32...) fusion(f32[32,4,255]{2,1,0:T(4,128)} %split.76, ...), kind=kLoop, calls=%fused_computation.90 | loop fusion | flops 293760 | bytes 2350335 | tf_op jit(solution)/shard_map/transpose(jvp(jit(_where)))/select_n | solution.py:54
  113.6 1.6 unstack.213
  116.9 1.6 unstack.211
  120.2 1.6 unstack.207
  121.8 1.6 copy.136
  123.4 1.6 unstack.205
  125.0 1.6 copy.135
  126.6 1.6 unstack.201
  128.2 1.6 copy.133
  130.5 1.6 copy.132
  140.6 1.1 pad_bitcast_fusion.6
  146.6 1.6 copy.112
  148.6 2.3 %fusion.41 = f32[864,512]{1,0:T(8,128)} fusion(bf16[864,1024]{1,0:T(8,128)(2,1)S(1)} %bitcast.644, bf16[512,1024]{1,0:T(8,128)(2,1)S(1)} %bitcast.639), kind=kOutput, calls=%fused_computation.301 | convolution fusion | flops 905969664 | bytes 4587520 | tf_op jit(solution)/shard_map/dot_general | solution.py:91
  153.4 4.9 %all-to-all-start.1 = ((bf16[32,8,4,256]{3,0,2,1:T(8,128)(2,1)}), bf16[32,8,4,256]{3,0,2,1:T(8,128)(2,1)S(1)}, u32[]{:S(2)}, u32[]{:S(2)}) async-start(bf16[32,8,4,256]{3,0,2,1:T(8,128)(2,1)} %bitcast.236), calls=%async_computation.1 | async-start | bytes 1048576 | tf_op jit(solution)/shard_map/all_to_all | solution.py:136
  158.6 15.0 %all-to-all-done.1 = bf16[32,8,4,256]{3,0,2,1:T(8,128)(2,1)S(1)} async-done(((bf16[32,8,4,256]{3,0,2,1:T(8,128)(2,1)}), bf16[32,8,4,256]{3,0,2,1:T(8,128)(2,1)S(1)}, u32[]{:S(2)}, u32[]{:S(2)}) %all-to-all-start.1) | async-done | bytes 524320 | tf_op jit(solution)/shard_map/all_to_all | solution.py:136
  174.2 1.2 copy.145
  175.4 41.1 %all-reduce.93.cloned.1.call-done = f32[3,3,3,32,512]{4,3,2,1,0:T(8,128)} async-done(((f32[3,3,3,32,512]{4,3,2,1,0:T(8,128)}), f32[3,3,3,32,512]{4,3,2,1,0:T(8,128)}) %all-reduce.93.cloned.1.call-update) | async-done | bytes 1769488 | tf_op jit(solution)/shard_map/psum | solution.py:126
  216.6 2.9 %copy.239 = f32[3,3,3,32,512]{4,3,2,1,0:T(8,128)} copy(f32[3,3,3,32,512]{4,3,2,1,0:T(8,128)} %all-reduce.93.cloned.1.call-done) | data formatting | bytes 3538944
  (203 shorter events, 28.6 us)
Async XLA Ops:
  7.2 38.4 %copy-start = (bf16[3,3,3,128,256]{4,3,2,1,0:T(8,128)(2,1)S(1)}, bf16[3,3,3,128,256]{4,3,2,1,0:T(8,128)(2,1)}, u32[]{:S(2)}) copy-start(bf16[3,3,3,128,256]{4,3,2,1,0:T(8,128)(2,1)} %param.5) | copy-start | bytes 5308420
  7.2 70.0 %all-gather.3.cloned.1.call-start = ((), (), s32[]{:S(2)}) async-start(), calls=%async_computation.3 | async-start | bytes 1179648 | tf_op jit(solution)/shard_map/all_gather | solution.py:122
  11.2 7.0 %collective-permute-start = (bf16[128,1,4,4,256]{4,0,3,2,1:T(8,128)(2,1)S(1)}, bf16[128,1,4,4,256]{4,0,3,2,1:T(8,128)(2,1)}, u32[]{:S(2)}, u32[]{:S(2)}) collective-permute-start(bf16[128,1,4,4,256]{4,0,3,2,1:T(8,128)(2,1)S(1)} %get-tuple-element.34), channel_id=1, source_target_pairs={{0,1},{1,2},{2,3},{3,4},{4,5},{5,6},{6,7},{8,9},{9,10},{10,11},{11... | collective-permute-start | bytes 3145736 | tf_op jit(solution)/shard_map/ppermute | solution.py:16
  52.8 25.8 %copy-start.2 = (bf16[3,3,3,32,512]{4,3,2,1,0:T(8,128)(2,1)S(1)}, bf16[3,3,3,32,512]{4,3,2,1,0:T(8,128)(2,1)}, u32[]{:S(2)}) copy-start(bf16[3,3,3,32,512]{4,3,2,1,0:T(8,128)(2,1)} %param.6) | copy-start | bytes 2654212
  52.8 91.6 %all-to-all-start = ((bf16[256,1,4,256]{3,2,1,0:T(4,128)(2,1)}), bf16[256,1,4,256]{3,2,1,0:T(4,128)(2,1)S(1)}, u32[]{:S(2)}, u32[]{:S(2)}) async-start(bf16[256,1,4,256]{3,2,1,0:T(4,128)(2,1)} %copy.105), calls=%async_computation | async-start | bytes 1048576 | tf_op jit(solution)/shard_map/all_to_all | solution.py:115
  77.0 139.6 %all-reduce.93.cloned.1.call-start = ((), (), s32[]{:S(2)}) async-start(), calls=%async_computation.2 | async-start | bytes 3538944 | tf_op jit(solution)/shard_map/psum | solution.py:126
  137.7 5.0 %copy-start.11 = (f32[32,4,224]{2,0,1:T(8,128)S(1)}, f32[32,4,224]{2,0,1:T(8,128)}, u32[]{:S(2)}) copy-start(f32[32,4,224]{2,0,1:T(8,128)} %copy.152) | copy-start | bytes 344068
  137.7 5.8 %copy-start.9 = (f32[32,4,255]{2,0,1:T(8,128)S(1)}, f32[32,4,255]{2,0,1:T(8,128)}, u32[]{:S(2)}) copy-start(f32[32,4,255]{2,0,1:T(8,128)} %get-tuple-element.143) | copy-start | bytes 391684
  137.7 5.8 %copy-start.10 = (f32[32,4,255]{2,0,1:T(8,128)S(1)}, f32[32,4,255]{2,0,1:T(8,128)}, u32[]{:S(2)}) copy-start(f32[32,4,255]{2,0,1:T(8,128)} %get-tuple-element.145) | copy-start | bytes 391684
  140.5 3.7 %copy-start.12 = (f32[32,4,1,1,256]{4,0,1,3,2:T(8,128)S(1)}, f32[32,4,1,1,256]{4,0,1,3,2:T(8,128)}, u32[]{:S(2)}) copy-start(f32[32,4,1,1,256]{4,0,1,3,2:T(8,128)} %pad_bitcast_fusion) | copy-start | bytes 393220
  140.5 3.7 %copy-start.13 = (f32[32,4,1,1,256]{4,0,1,3,2:T(8,128)S(1)}, f32[32,4,1,1,256]{4,0,1,3,2:T(8,128)}, u32[]{:S(2)}) copy-start(f32[32,4,1,1,256]{4,0,1,3,2:T(8,128)} %copy.136) | copy-start | bytes 393220
  140.5 3.7 %copy-start.14 = (f32[32,4,1,1,256]{4,0,1,3,2:T(8,128)S(1)}, f32[32,4,1,1,256]{4,0,1,3,2:T(8,128)}, u32[]{:S(2)}) copy-start(f32[32,4,1,1,256]{4,0,1,3,2:T(8,128)} %copy.135) | copy-start | bytes 393220
  140.5 3.7 %copy-start.15 = (f32[32,4,1,1,256]{4,0,1,3,2:T(8,128)S(1)}, f32[32,4,1,1,256]{4,0,1,3,2:T(8,128)}, u32[]{:S(2)}) copy-start(f32[32,4,1,1,256]{4,0,1,3,2:T(8,128)} %copy.133) | copy-start | bytes 393220
  140.5 3.7 %copy-start.16 = (f32[32,4,1,1,256]{4,0,1,3,2:T(8,128)S(1)}, f32[32,4,1,1,256]{4,0,1,3,2:T(8,128)}, u32[]{:S(2)}) copy-start(f32[32,4,1,1,256]{4,0,1,3,2:T(8,128)} %copy.132) | copy-start | bytes 393220
  151.0 0.9 copy-start.4
  151.0 1.3 copy-start.5
  151.0 1.4 copy-start.6
  151.0 1.4 copy-start.7
  151.0 1.4 copy-start.8
  152.5 5.8 %copy-start.3 = (f32[1024,256]{1,0:T(8,128)S(1)}, f32[1024,256]{1,0:T(8,128)}, u32[]{:S(2)}) copy-start(f32[1024,256]{1,0:T(8,128)} %get-tuple-element.168) | copy-start | bytes 3145732
  153.4 20.2 %all-to-all-start.1 = ((bf16[32,8,4,256]{3,0,2,1:T(8,128)(2,1)}), bf16[32,8,4,256]{3,0,2,1:T(8,128)(2,1)S(1)}, u32[]{:S(2)}, u32[]{:S(2)}) async-start(bf16[32,8,4,256]{3,0,2,1:T(8,128)(2,1)} %bitcast.236), calls=%async_computation.1 | async-start | bytes 1048576 | tf_op jit(solution)/shard_map/all_to_all | solution.py:136
  174.2 45.2 %copy-start.1 = (bf16[3,3,3,128,256]{4,3,2,1,0:T(8,128)(2,1)S(1)}, bf16[3,3,3,128,256]{4,3,2,1,0:T(8,128)(2,1)}, u32[]{:S(2)}) copy-start(bf16[3,3,3,128,256]{4,3,2,1,0:T(8,128)(2,1)} %param.5) | copy-start | bytes 5308420
Sparse Core Ops, SparseCore 0:
  14.8 24.9 all-gather.2
  151.1 65.3 all-reduce.92
where the time goes:
time: 228 us; the launch traced here: 226 us
  local copies, waits for them, and re-layouts  107 us (47%)
  waiting for transfers between devices  56.2 us (25%)
  starting transfers between devices  32.6 us (14%)
  between operations  15.4 us (7%)
  matrix products  9.61 us (4%)
  other arithmetic  5.63 us (2%)
    psum x1, waiting for transfers between devices, per_device(): grad_second = lax.psum(weight_grad, 'dp').reshape(3, 3, 3, own_channels, C3)  41.1 us
    all_to_all x1, starting transfers between devices, per_device(): lax.all_to_all(hidden, 'space', split_axis=0, concat_axis=1, tiled=True)  24.1 us
    another operation x26, local copies, waits for them, and re-layouts, plane_taps(): rows_out.append(jnp.stack(cols_out, -2))  21.4 us
    reshape x1, local copies, waits for them, and re-layouts, per_device(): stacked = jnp.stack(collected, 0).reshape(27 * channels, -1)  16.2 us
    all_to_all x1, waiting for transfers between devices, per_device(): lax.all_to_all(back_terms, 'space', split_axis=1, concat_axis=0, tiled=True)  15 us
    split x10, local copies, waits for them, and re-layouts, step_cells(): moved = jnp.concatenate([filler, values[..., :cells - 1]], -1)  14.6 us
    unnamed x62, local copies, waits for them, and re-layouts  14.5 us
    another operation x26, local copies, waits for them, and re-layouts, spread(): return jnp.stack(all_taps(field, row_len), 0).reshape(27 * own_channels, -1)  14.4 us
  transfers between devices with their start and end apart: 5, of which 2 were waited for; matrix products, arithmetic and copies ran while one was open for 48% of the time, Pallas kernels for 0%

commit v1 on v0

--- a/solution.py
+++ b/solution.py
@@ -1,6 +1,10 @@
+import functools
+
 import jax
 import jax.numpy as jnp
 from jax import lax
+from jax.experimental import pallas as pl
+from jax.experimental.pallas import tpu as pltpu
 from jax.sharding import PartitionSpec as P
 
 C3 = 512
@@ -93,7 +97,7 @@
     )
 
 
-def per_device(volume, w_first, w_second, cotangent):
+def plain_device(volume, w_first, w_second, cotangent):
     channels = volume.shape[1]
     depth_cells = volume.shape[2]
     cell_count = volume.shape[4]
@@ -138,6 +142,348 @@
     return (grad_second, pre_grad[None])
 
 
+def moved_cells(block, by_row, by_col, row_len):
+    if not (by_row or by_col):
+        return block
+    cells = block.shape[-1]
+    at = lax.broadcasted_iota(jnp.int32, block.shape, 1)
+    wide = block.astype(jnp.float32)
+    if by_row:
+        wide = jnp.where(at >= row_len, pltpu.roll(wide, row_len, 1), 0.0)
+    if by_col:
+        wide = jnp.where(at % row_len != 0, pltpu.roll(wide, 1, 1), 0.0)
+    return wide.astype(block.dtype)
+
+
+def moved_back(block, by_row, by_col, row_len):
+    cells = block.shape[-1]
+    at = lax.broadcasted_iota(jnp.int32, block.shape, 1)
+    if by_row:
+        block = pltpu.roll(jnp.where(at >= row_len, block, 0.0), cells - row_len, 1)
+    if by_col:
+        block = pltpu.roll(jnp.where(at % row_len != 0, block, 0.0), cells - 1, 1)
+    return block
+
+
+def fill_taps(plane, taps, row_len):
+    _, channels, cells = plane.shape
+    for row_tap in range(3):
+        for col_tap in range(3):
+            top = (row_tap * 3 + col_tap) * channels
+            for row_phase in range(2):
+                for col_phase in range(2):
+                    row_at = 2 * row_phase + row_tap - 1
+                    col_at = 2 * col_phase + col_tap - 1
+                    part = plane[(row_at % 4) * 4 + col_at % 4]
+                    left = (row_phase * 2 + col_phase) * cells
+                    taps[top : top + channels, left : left + cells] = moved_cells(
+                        part, row_at < 0, col_at < 0, row_len
+                    )
+
+
+def greet(axes):
+    barrier = pltpu.get_barrier_semaphore()
+    total = 0
+    for axis, size in axes:
+        me = lax.axis_index(axis)
+        for k in range(1, size):
+            pl.semaphore_signal(
+                barrier, inc=1, device_id={axis: (me + k) % size}, device_id_type=pl.DeviceIdType.MESH
+            )
+        total += size - 1
+    pl.semaphore_wait(barrier, total)
+
+
+def to_device(src, dst, send_sem, recv_sem, axis, peer):
+    return pltpu.make_async_remote_copy(
+        src_ref=src,
+        dst_ref=dst,
+        send_sem=send_sem,
+        recv_sem=recv_sem,
+        device_id={axis: peer},
+        device_id_type=pl.DeviceIdType.MESH,
+    )
+
+
+def first_kernel(
+    n, row_len, chunks,
+    vol, w, pre, hid_out,
+    taps, part, rim, hid_send, hid_recv, rim_send_sem, rim_recv_sem, send_sem, recv_sem,
+):
+    me = lax.axis_index("space")
+    channels = vol.shape[2]
+    rows = 9 * channels
+    out_channels = w.shape[1]
+    wide = out_channels // chunks
+    group = out_channels // n
+    per_chunk = n // chunks
+    greet([("space", n)])
+
+    fill_taps(vol.at[1], taps, row_len)
+
+    def rim_copy(c):
+        cut = pl.ds(c * wide, wide)
+        return to_device(
+            part.at[cut], rim.at[cut], rim_send_sem.at[c], rim_recv_sem.at[c], "space", (me + 1) % n
+        )
+
+    for c in range(chunks):
+        cut = slice(c * wide, (c + 1) * wide)
+        part[cut, :] = contract_first(w[0:rows, cut], taps[...]).astype(part.dtype)
+
+        @pl.when(me < n - 1)
+        def _():
+            rim_copy(c).start()
+
+    pre[...] = contract_first(w[2 * rows : 3 * rows, :], taps[...])
+    fill_taps(vol.at[0], taps, row_len)
+    pre[...] += contract_first(w[rows : 2 * rows, :], taps[...])
+
+    def hid_copy(peer):
+        return to_device(
+            hid_send.at[peer], hid_recv.at[me], send_sem.at[peer], recv_sem.at[me], "space", peer
+        )
+
+    def hid_arrival(source):
+        return to_device(
+            hid_send.at[source], hid_recv.at[source], send_sem.at[source], recv_sem.at[source], "space", source
+        )
+
+    for c in range(chunks):
+        cut = slice(c * wide, (c + 1) * wide)
+
+        @pl.when(me > 0)
+        def _():
+            rim_copy(c).wait_recv()
+            pre[cut, :] += rim[cut, :].astype(jnp.float32)
+
+        for g in range(per_chunk):
+            at = c * per_chunk + g
+            hid_send[at] = activate(pre[at * group : (at + 1) * group, :]).astype(hid_send.dtype)
+        for k in range(per_chunk):
+            peer = c * per_chunk + (me + k + 1) % per_chunk
+
+            @pl.when(peer != me)
+            def _():
+                hid_copy(peer).start()
+
+    for k in range(1, n):
+        hid_arrival((me + k) % n).wait_recv()
+    hid_recv[me] = hid_send[me]
+    hid_out[...] = hid_recv[...]
+    for k in range(1, n):
+        hid_copy((me + k) % n).wait_send()
+
+    @pl.when(me < n - 1)
+    def _():
+        for c in range(chunks):
+            rim_copy(c).wait_send()
+
+
+def second_kernel(
+    n, m, row_len,
+    hid, w, cot, grad, back_out,
+    taps, terms, back_send, back_recv, sum_send, sum_recv, all_send, all_recv,
+    back_send_sem, back_recv_sem, sum_send_sem, sum_recv_sem, all_send_sem, all_recv_sem,
+):
+    me = lax.axis_index("space")
+    mine = lax.axis_index("dp")
+    depth, group, _ = hid.shape
+    cells = row_len * (hid.shape[2] // 4 // row_len)
+    planes = depth // 2
+    quarter = cot.shape[0] // m
+    greet([("space", n), ("dp", m)])
+
+    def cell_block(a, b, c, s):
+        top = ((a * 3 + b) * 3 + c) * group
+        return (slice(top, top + group), slice(s * cells, (s + 1) * cells))
+
+    for x in range(depth):
+        for b in range(3):
+            for c in range(3):
+                phase = 2 * ((b + 1) % 2) + (c + 1) % 2
+                value = moved_cells(
+                    hid[x, :, phase * cells : (phase + 1) * cells], b == 0, c == 0, row_len
+                )
+                if x % 2 == 0:
+                    taps[cell_block(1, b, c, x // 2)] = value
+                else:
+                    taps[cell_block(2, b, c, x // 2)] = value
+                    if x // 2 + 1 < planes:
+                        taps[cell_block(0, b, c, x // 2 + 1)] = value
+                if x == 0:
+                    taps[cell_block(0, b, c, 0)] = jnp.zeros_like(value)
+
+    def sum_copy(peer):
+        return to_device(
+            sum_send.at[peer], sum_recv.at[mine], sum_send_sem.at[peer], sum_recv_sem.at[mine], "dp", peer
+        )
+
+    def all_copy(peer):
+        return to_device(
+            all_send, all_recv.at[mine], all_send_sem.at[peer], all_recv_sem.at[mine], "dp", peer
+        )
+
+    def quarter_of(owner):
+        cut = pl.ds(pl.multiple_of(owner * quarter, quarter), quarter)
+        return contract_last(taps[...], cot[cut, :])
+
+    for k in range(1, m):
+        peer = (mine + k) % m
+        sum_send[peer] = quarter_of(peer).astype(sum_send.dtype)
+        sum_copy(peer).start()
+
+    terms[...] = jnp.dot(w[...], cot[...], preferred_element_type=jnp.float32)
+
+    def term(x, b, c):
+        if x % 2 == 0:
+            return terms[cell_block(1, b, c, x // 2)]
+        value = terms[cell_block(2, b, c, x // 2)]
+        if x // 2 + 1 < planes:
+            value = value + terms[cell_block(0, b, c, x // 2 + 1)]
+        return value
+
+    def back_copy(peer):
+        return to_device(
+            back_send.at[peer], back_recv.at[me], back_send_sem.at[peer], back_recv_sem.at[me], "space", peer
+        )
+
+    for x in range(depth):
+        corner = term(x, 0, 2) + moved_back(term(x, 0, 0), False, True, row_len)
+        phases = [
+            term(x, 1, 1),
+            term(x, 1, 2) + moved_back(term(x, 1, 0), False, True, row_len),
+            term(x, 2, 1) + moved_back(term(x, 0, 1), True, False, row_len),
+            term(x, 2, 2)
+            + moved_back(term(x, 2, 0), False, True, row_len)
+            + moved_back(corner, True, False, row_len),
+        ]
+        for phase in range(4):
+            back_send[x, :, phase * cells : (phase + 1) * cells] = phases[phase].astype(back_send.dtype)
+    for k in range(1, n):
+        back_copy((me + k) % n).start()
+
+    own = quarter_of(mine)
+    own_cut = pl.ds(pl.multiple_of(mine * quarter, quarter), quarter)
+    for k in range(1, m):
+        source = (mine + k) % m
+        to_device(
+            sum_send.at[source], sum_recv.at[source], sum_send_sem.at[source], sum_recv_sem.at[source], "dp", source
+        ).wait_recv()
+        own = own + sum_recv[source].astype(jnp.float32)
+    grad[:, own_cut] = own
+    all_send[...] = own.astype(all_send.dtype)
+    for k in range(1, m):
+        all_copy((mine + k) % m).start()
+
+    back_recv[me] = back_send[me]
+    for k in range(1, n):
+        source = (me + k) % n
+        to_device(
+            back_send.at[source], back_recv.at[source], back_send_sem.at[source], back_recv_sem.at[source], "space", source
+        ).wait_recv()
+    back_out[...] = back_recv[...]
+    for k in range(1, m):
+        source = (mine + k) % m
+        to_device(
+            all_send, all_recv.at[source], all_send_sem.at[source], all_recv_sem.at[source], "dp", source
+        ).wait_recv()
+        cut = pl.ds(pl.multiple_of(source * quarter, quarter), quarter)
+        grad[:, cut] = all_recv[source].astype(jnp.float32)
+    for k in range(1, n):
+        back_copy((me + k) % n).wait_send()
+    for k in range(1, m):
+        sum_copy((mine + k) % m).wait_send()
+        all_copy((mine + k) % m).wait_send()
+
+
+def in_vmem(count):
+    return [pl.BlockSpec(memory_space=pltpu.VMEM)] * count
+
+
+def per_device(volume, w_first, w_second, cotangent):
+    n = lax.axis_size("space")
+    m = lax.axis_size("dp")
+    channels = volume.shape[1]
+    cells = volume.shape[4]
+    out_channels = w_first.shape[4]
+    group = w_second.shape[3]
+    last = w_second.shape[4]
+    row_len = WID // 4
+    if volume.shape[2] != 2 or group % 16 or (last // m) % 128 or n % 2:
+        return plain_device(volume, w_first, w_second, cotangent)
+    planes = jnp.transpose(volume[0], (1, 2, 0, 3))
+    w_flat = w_first.reshape(27 * channels, out_channels)
+    span = 4 * cells
+    chunks = 2
+    pre, hidden = pl.pallas_call(
+        functools.partial(first_kernel, n, row_len, chunks),
+        out_shape=(
+            jax.ShapeDtypeStruct((out_channels, span), jnp.float32),
+            jax.ShapeDtypeStruct((n, group, span), jnp.bfloat16),
+        ),
+        in_specs=in_vmem(2),
+        out_specs=tuple(in_vmem(2)),
+        scratch_shapes=[
+            pltpu.VMEM((9 * channels, span), jnp.bfloat16),
+            pltpu.VMEM((out_channels, span), jnp.bfloat16),
+            pltpu.VMEM((out_channels, span), jnp.bfloat16),
+            pltpu.VMEM((n, group, span), jnp.bfloat16),
+            pltpu.VMEM((n, group, span), jnp.bfloat16),
+            pltpu.SemaphoreType.DMA((chunks,)),
+            pltpu.SemaphoreType.DMA((chunks,)),
+            pltpu.SemaphoreType.DMA((n,)),
+            pltpu.SemaphoreType.DMA((n,)),
+        ],
+        compiler_params=pltpu.CompilerParams(
+            collective_id=0, has_side_effects=True, vmem_limit_bytes=40 * 2**20
+        ),
+        cost_estimate=pl.CostEstimate(
+            flops=2 * 27 * channels * out_channels * span, bytes_accessed=6 * 2**20, transcendentals=0
+        ),
+    )(planes, w_flat)
+    cot = lax.all_gather(cotangent[0].reshape(cotangent.shape[1], -1), "space", axis=0, tiled=True)
+    rows = 27 * group
+    out_cells = cot.shape[1]
+    grad, back = pl.pallas_call(
+        functools.partial(second_kernel, n, m, row_len),
+        out_shape=(
+            jax.ShapeDtypeStruct((rows, last), jnp.float32),
+            jax.ShapeDtypeStruct((n, group, span), jnp.bfloat16),
+        ),
+        in_specs=in_vmem(3),
+        out_specs=tuple(in_vmem(2)),
+        scratch_shapes=[
+            pltpu.VMEM((rows, out_cells), jnp.bfloat16),
+            pltpu.VMEM((rows, out_cells), jnp.float32),
+            pltpu.VMEM((n, group, span), jnp.bfloat16),
+            pltpu.VMEM((n, group, span), jnp.bfloat16),
+            pltpu.VMEM((m, rows, last // m), jnp.bfloat16),
+            pltpu.VMEM((m, rows, last // m), jnp.bfloat16),
+            pltpu.VMEM((rows, last // m), jnp.bfloat16),
+            pltpu.VMEM((m, rows, last // m), jnp.bfloat16),
+            pltpu.SemaphoreType.DMA((n,)),
+            pltpu.SemaphoreType.DMA((n,)),
+            pltpu.SemaphoreType.DMA((m,)),
+            pltpu.SemaphoreType.DMA((m,)),
+            pltpu.SemaphoreType.DMA((m,)),
+            pltpu.SemaphoreType.DMA((m,)),
+        ],
+        compiler_params=pltpu.CompilerParams(
+            collective_id=1, has_side_effects=True, vmem_limit_bytes=40 * 2**20
+        ),
+        cost_estimate=pl.CostEstimate(
+            flops=4 * rows * last * out_cells, bytes_accessed=6 * 2**20, transcendentals=0
+        ),
+    )(hidden, w_second.reshape(rows, last), cot)
+    hidden_grad = back.reshape(out_channels, span)
+    pre_grad = (hidden_grad.astype(jnp.float32) * slope_of(pre)).astype(jnp.bfloat16)
+    return (
+        grad.reshape(3, 3, 3, group, last),
+        pre_grad.reshape(1, out_channels, 1, 4, cells),
+    )
+
+
 def solution(mesh):
     in_specs = (
         P("dp", None, "space", None, None),

time: 228 us -> 85.8 us (0.38)
  local copies, waits for them, and re-layouts: 107 us -> 9.24 us
  Pallas kernels: 0 us -> 61.7 us
  waiting for transfers between devices: 56.2 us -> 0.04 us
  starting transfers between devices: 32.6 us -> 0.04 us
  matrix products: 9.61 us -> 0 us
  other arithmetic: 5.63 us -> 0.51 us
    pallas_call x0 -> x2, Pallas kernels: none -> 61.7 us  [the longest x1 32.2 us: per_device(): pl.pallas_call(functools.partial(second_kernel, n, m, row_len), out_shape...]
    another operation x55 -> x0, local copies, waits for them, and re-layouts: 44.2 us -> none  [the longest x26 21.4 us: plane_taps(): rows_out.append(jnp.stack(cols_out, -2))]
    psum x1 -> x0, waiting for transfers between devices: 41.1 us -> none  [per_device(): grad_second = lax.psum(weight_grad, 'dp').reshape(3, 3, 3, own_channels, C3)]
    all_to_all x2 -> x0, starting transfers between devices: 29 us -> none  [the longest x1 24.1 us: per_device(): lax.all_to_all(hidden, 'space', split_axis=0, concat_axis=1, tiled=True)]
    split x18 -> x0, local copies, waits for them, and re-layouts: 18.9 us -> none  [the longest x10 14.6 us: step_cells(): moved = jnp.concatenate([filler, values[..., :cells - 1]], -1)]
    reshape x2 -> x1, local copies, waits for them, and re-layouts: 16.5 us -> 1.17 us  [per_device(): pre_grad.reshape(1, out_channels, 1, 4, cells)]
    all_to_all x2 -> x0, waiting for transfers between devices: 15 us -> none  [the longest x1 15 us: per_device(): lax.all_to_all(back_terms, 'space', split_axis=1, concat_axis=0, tiled=True)]
    dot_general x3 -> x0, matrix products: 9.61 us -> none  [the longest x1 6.2 us: contract_first(): lax.dot_general(left_side, right_side, (((0,), (0,)), ((), ())), preferre...]
  transfers between devices with their start and end apart: 5 -> 1, of which waited for: 2 -> 0; matrix products, arithmetic and copies ran while one was open for 48% -> 3% of each run, Pallas kernels for 0% -> 34%
where the time goes in v1:
time: 85.8 us; the launch traced here: 85.6 us
  Pallas kernels  61.7 us (72%)
  between operations  14.1 us (16%)
  local copies, waits for them, and re-layouts  9.24 us (11%)
    pallas_call x1, Pallas kernels, per_device(): pl.pallas_call(functools.partial(second_kernel, n, m, row_len), out_shape...  32.2 us
    pallas_call x1, Pallas kernels, per_device(): pl.pallas_call(functools.partial(first_kernel, n, row_len, chunks), out_s...  29.5 us
    unnamed x9, local copies, waits for them, and re-layouts  8.07 us
  transfers between devices with their start and end apart: 1, of which 0 were waited for; matrix products, arithmetic and copies ran while one was open for 3% of the time, Pallas kernels for 34%

profile of v1, /device:TPU:0, one launch (start us, length us, event | category | flops | bytes accessed | tf_op | source)
XLA Modules:
  0.0 85.6 jit_solution(7265332705872995659)
XLA Ops:
  7.2 0.0 all-gather.2.cloned.1.call-start
  7.2 1.6 %copy.8 = bf16[8,8,4,256]{3,1,2,0:T(8,128)(2,1)} copy(bf16[8,8,4,256]{3,2,1,0:T(4,128)(2,1)} %bitcast.21) | data formatting | bytes 262144
  8.8 0.0 all-gather.2.cloned.1.call-update
  8.8 0.0 copy-start
  8.8 2.9 %copy.10 = bf16[1,128,2,16,256]{4,1,3,2,0:T(8,128)(2,1)S(1)} copy(bf16[1,128,2,16,256]{4,3,2,1,0:T(8,128)(2,1)} %param.4) | data formatting | bytes 4194304 | tf_op args[0]
  11.7 0.0 copy-done
  11.7 29.5 %shard_map.59 = (f32[256,1024]{1,0:T(8,128)S(1)}, bf16[8,32,1024]{2,1,0:T(8,128)(2,1)S(1)}) custom-call(bf16[2,16,128,256]{3,2,1,0:T(8,128)(2,1)S(1)} %bitcast.15, bf16[3456,256]{1,0:T(8,128)(2,1)S(1)} %bitcast.17), custom_call_target="tpu_custom_call" | custom-call | flops 1811939328 | bytes 6291456 | tf_op jit(solution)/shard_map/pallas_call | solution.py:419
  41.2 0.0 all-gather.2.cloned.1.call-done.cot
  41.3 0.0 copy-start.1
  41.3 1.2 %copy-done.1 = bf16[512,1024]{1,0:T(8,128)(2,1)S(1)} copy-done((bf16[512,1024]{1,0:T(8,128)(2,1)S(1)}, bf16[512,1024]{1,0:T(8,128)(2,1)}, u32[]{:S(2)}) %copy-start.1) | copy-done | bytes 1048600
  42.5 0.0 copy-start.2
  42.5 1.2 %copy-done.2 = bf16[3,3,3,32,512]{4,3,2,1,0:T(8,128)(2,1)S(1)} copy-done((bf16[3,3,3,32,512]{4,3,2,1,0:T(8,128)(2,1)S(1)}, bf16[3,3,3,32,512]{4,3,2,1,0:T(8,128)(2,1)}, u32[]{:S(2)}) %copy-start.2) | copy-done | bytes 884760
  43.7 32.2 %shard_map.60 = (f32[864,512]{1,0:T(8,128)S(1)}, bf16[8,32,1024]{2,1,0:T(8,128)(2,1)S(1)}) custom-call(bf16[8,32,1024]{2,1,0:T(8,128)(2,1)S(1)} %get-tuple-element.6.hid, bf16[864,512]{1,0:T(8,128)(2,1)S(1)} %bitcast.18, bf16[512,1024]{1,0:T(8,128)(2,1)S(1)} %copy-done.1), custom_call_target="tpu_custom_call" | custom-call | flops 1811939328 | bytes 6291456 | tf_op jit(solution)/shard_map/pallas_call | solution.py:448
  75.8 0.5 fusion
  76.4 1.2 %reshape.22 = bf16[1,256,1,4,256]{4,3,1,2,0:T(4,128)(2,1)} reshape(bf16[256,1024]{1,0:T(8,128)(2,1)S(1)} %fusion) | data formatting | bytes 1048576 | tf_op jit(solution)/shard_map/reshape | solution.py:483
  77.5 1.2 %copy.12 = f32[3,3,3,32,512]{4,3,2,1,0:T(8,128)} copy(f32[3,3,3,32,512]{4,3,2,1,0:T(8,128)S(1)} %bitcast.16) | data formatting | bytes 3538944
Async XLA Ops:
  7.2 34.1 %all-gather.2.cloned.1.call-start = ((), (), s32[]{:S(2)}) async-start(), calls=%async_computation | async-start | bytes 1179648 | tf_op jit(solution)/shard_map/all_gather | solution.py:445
  8.8 2.9 %copy-start = (bf16[3,3,3,128,256]{4,3,2,1,0:T(8,128)(2,1)S(1)}, bf16[3,3,3,128,256]{4,3,2,1,0:T(8,128)(2,1)}, u32[]{:S(2)}) copy-start(bf16[3,3,3,128,256]{4,3,2,1,0:T(8,128)(2,1)} %param.5) | copy-start | bytes 5308420
  41.3 1.2 %copy-start.1 = (bf16[512,1024]{1,0:T(8,128)(2,1)S(1)}, bf16[512,1024]{1,0:T(8,128)(2,1)}, u32[]{:S(2)}) copy-start(bf16[512,1024]{1,0:T(8,128)(2,1)} %all-gather.2.cloned.1.call-done.cot) | copy-start | bytes 3145732
  42.5 1.2 %copy-start.2 = (bf16[3,3,3,32,512]{4,3,2,1,0:T(8,128)(2,1)S(1)}, bf16[3,3,3,32,512]{4,3,2,1,0:T(8,128)(2,1)}, u32[]{:S(2)}) copy-start(bf16[3,3,3,32,512]{4,3,2,1,0:T(8,128)(2,1)} %param.6) | copy-start | bytes 2654212
Sparse Core Ops, SparseCore 0:
  10.2 30.8 all-gather.1

commit v2 on v1

--- a/solution.py
+++ b/solution.py
@@ -205,21 +205,85 @@
     )
 
 
-def first_kernel(
-    n, row_len, chunks,
-    vol, w, pre, hid_out,
-    taps, part, rim, hid_send, hid_recv, rim_send_sem, rim_recv_sem, send_sem, recv_sem,
+def section_kernel(
+    n, m, row_len, chunks,
+    vol, w1_hbm, w2_hbm, cot_own, grad, pre_grad,
+    w1, w2, cot, taps, pre, part, rim, hid_send, hid_recv,
+    out_taps, terms, back_send, back_recv, sum_send, sum_recv, all_send, all_recv,
+    w1_sem, w2_sem, cot_send_sem, cot_recv_sem, rim_send_sem, rim_recv_sem, hid_send_sem, hid_recv_sem,
+    back_send_sem, back_recv_sem, sum_send_sem, sum_recv_sem, all_send_sem, all_recv_sem,
 ):
     me = lax.axis_index("space")
+    mine = lax.axis_index("dp")
+    chips = n // 2
+    chip = me // 2
+    core = me % 2
     channels = vol.shape[2]
+    cells = vol.shape[3]
     rows = 9 * channels
-    out_channels = w.shape[1]
+    out_channels = w1.shape[1]
     wide = out_channels // chunks
     group = out_channels // n
     per_chunk = n // chunks
-    greet([("space", n)])
+    depth = n
+    planes = depth // 2
+    quarter = cot.shape[0] // m
+    share = cot_own.shape[0]
+
+    def w1_copy(a):
+        cut = pl.ds(a * rows, rows)
+        return pltpu.make_async_copy(w1_hbm.at[cut], w1.at[cut], w1_sem.at[a])
+
+    for a in (0, 2, 1):
+        w1_copy(a).start()
+    w2_copy = pltpu.make_async_copy(w2_hbm, w2, w2_sem.at[0])
+    w2_copy.start()
+    own_rows = pl.ds(pl.multiple_of(me * share, share), share)
+    for s in range(planes):
+        cot[own_rows, s * cells : (s + 1) * cells] = cot_own[:, s, :]
+    greet([("space", n), ("dp", m)])
+
+    def cot_copy(block, way):
+        cut = pl.ds(pl.multiple_of(block * share, share), share)
+        peer = [(me + 2) % n, (me + n - 2) % n, 2 * chip + 1 - core][way]
+        return to_device(
+            cot.at[cut], cot.at[cut], cot_send_sem.at[way, block], cot_recv_sem.at[block], "space", peer
+        )
+
+    def cot_send(h, act):
+        up = 2 * ((chip - h + chips) % chips) + core
+        down = 2 * ((chip + h) % chips) + core
+
+        @pl.when((chip - h >= 0) & (chip + 1 < chips))
+        def _():
+            act(cot_copy(up, 0))
+
+        @pl.when((chip + h < chips) & (chip - 1 >= 0))
+        def _():
+            act(cot_copy(down, 1))
+
+    def cot_pass(h, wait, act):
+        up = 2 * ((chip - h + chips) % chips) + core
+        down = 2 * ((chip + h) % chips) + core
+
+        @pl.when(chip - h >= 0)
+        def _():
+            if wait:
+                cot_copy(up, 2).wait_recv()
+            act(cot_copy(up, 2))
+
+        @pl.when(chip + h < chips)
+        def _():
+            if wait:
+                cot_copy(down, 2).wait_recv()
+            act(cot_copy(down, 2))
+
+    start = lambda copy: copy.start()
+    cot_copy(me, 2).start()
+    cot_send(0, start)
 
     fill_taps(vol.at[1], taps, row_len)
+    w1_copy(0).wait()
 
     def rim_copy(c):
         cut = pl.ds(c * wide, wide)
@@ -229,24 +293,24 @@
 
     for c in range(chunks):
         cut = slice(c * wide, (c + 1) * wide)
-        part[cut, :] = contract_first(w[0:rows, cut], taps[...]).astype(part.dtype)
+        part[cut, :] = contract_first(w1[0:rows, cut], taps[...]).astype(part.dtype)
 
         @pl.when(me < n - 1)
         def _():
             rim_copy(c).start()
 
-    pre[...] = contract_first(w[2 * rows : 3 * rows, :], taps[...])
+    w1_copy(2).wait()
+    pre[...] = contract_first(w1[2 * rows : 3 * rows, :], taps[...])
     fill_taps(vol.at[0], taps, row_len)
-    pre[...] += contract_first(w[rows : 2 * rows, :], taps[...])
+    w1_copy(1).wait()
+    pre[...] += contract_first(w1[rows : 2 * rows, :], taps[...])
+
+    cot_pass(1, True, start)
+    cot_send(1, start)
 
     def hid_copy(peer):
         return to_device(
-            hid_send.at[peer], hid_recv.at[me], send_sem.at[peer], recv_sem.at[me], "space", peer
-        )
-
-    def hid_arrival(source):
-        return to_device(
-            hid_send.at[source], hid_recv.at[source], send_sem.at[source], recv_sem.at[source], "space", source
+            hid_send.at[peer], hid_recv.at[me], hid_send_sem.at[peer], hid_recv_sem.at[me], "space", peer
         )
 
     for c in range(chunks):
@@ -267,73 +331,20 @@
             def _():
                 hid_copy(peer).start()
 
-    for k in range(1, n):
-        hid_arrival((me + k) % n).wait_recv()
+    for h in range(2, chips):
+        cot_pass(h, True, start)
+        if h + 1 < chips:
+            cot_send(h, start)
     hid_recv[me] = hid_send[me]
-    hid_out[...] = hid_recv[...]
-    for k in range(1, n):
-        hid_copy((me + k) % n).wait_send()
-
-    @pl.when(me < n - 1)
-    def _():
-        for c in range(chunks):
-            rim_copy(c).wait_send()
-
-
-def second_kernel(
-    n, m, row_len,
-    hid, w, cot, grad, back_out,
-    taps, terms, back_send, back_recv, sum_send, sum_recv, all_send, all_recv,
-    back_send_sem, back_recv_sem, sum_send_sem, sum_recv_sem, all_send_sem, all_recv_sem,
-):
-    me = lax.axis_index("space")
-    mine = lax.axis_index("dp")
-    depth, group, _ = hid.shape
-    cells = row_len * (hid.shape[2] // 4 // row_len)
-    planes = depth // 2
-    quarter = cot.shape[0] // m
-    greet([("space", n), ("dp", m)])
+    for z in range(chips):
+        cot_copy(2 * z + 1 - core, 2).wait_recv()
 
     def cell_block(a, b, c, s):
         top = ((a * 3 + b) * 3 + c) * group
         return (slice(top, top + group), slice(s * cells, (s + 1) * cells))
 
-    for x in range(depth):
-        for b in range(3):
-            for c in range(3):
-                phase = 2 * ((b + 1) % 2) + (c + 1) % 2
-                value = moved_cells(
-                    hid[x, :, phase * cells : (phase + 1) * cells], b == 0, c == 0, row_len
-                )
-                if x % 2 == 0:
-                    taps[cell_block(1, b, c, x // 2)] = value
-                else:
-                    taps[cell_block(2, b, c, x // 2)] = value
-                    if x // 2 + 1 < planes:
-                        taps[cell_block(0, b, c, x // 2 + 1)] = value
-                if x == 0:
-                    taps[cell_block(0, b, c, 0)] = jnp.zeros_like(value)
-
-    def sum_copy(peer):
-        return to_device(
-            sum_send.at[peer], sum_recv.at[mine], sum_send_sem.at[peer], sum_recv_sem.at[mine], "dp", peer
-        )
-
-    def all_copy(peer):
-        return to_device(
-            all_send, all_recv.at[mine], all_send_sem.at[peer], all_recv_sem.at[mine], "dp", peer
-        )
-
-    def quarter_of(owner):
-        cut = pl.ds(pl.multiple_of(owner * quarter, quarter), quarter)
-        return contract_last(taps[...], cot[cut, :])
-
-    for k in range(1, m):
-        peer = (mine + k) % m
-        sum_send[peer] = quarter_of(peer).astype(sum_send.dtype)
-        sum_copy(peer).start()
-
-    terms[...] = jnp.dot(w[...], cot[...], preferred_element_type=jnp.float32)
+    w2_copy.wait()
+    terms[...] = jnp.dot(w2[...], cot[...], preferred_element_type=jnp.float32)
 
     def term(x, b, c):
         if x % 2 == 0:
@@ -362,43 +373,90 @@
             back_send[x, :, phase * cells : (phase + 1) * cells] = phases[phase].astype(back_send.dtype)
     for k in range(1, n):
         back_copy((me + k) % n).start()
-
-    own = quarter_of(mine)
-    own_cut = pl.ds(pl.multiple_of(mine * quarter, quarter), quarter)
+    back_recv[me] = back_send[me]
+
+    for k in range(1, n):
+        source = (me + k) % n
+        to_device(
+            hid_send.at[source], hid_recv.at[source], hid_send_sem.at[source], hid_recv_sem.at[source], "space", source
+        ).wait_recv()
+    for x in range(depth):
+        for b in range(3):
+            for c in range(3):
+                phase = 2 * ((b + 1) % 2) + (c + 1) % 2
+                value = moved_cells(
+                    hid_recv[x, :, phase * cells : (phase + 1) * cells], b == 0, c == 0, row_len
+                )
+                if x % 2 == 0:
+                    out_taps[cell_block(1, b, c, x // 2)] = value
+                else:
+                    out_taps[cell_block(2, b, c, x // 2)] = value
+                    if x // 2 + 1 < planes:
+                        out_taps[cell_block(0, b, c, x // 2 + 1)] = value
+                if x == 0:
+                    out_taps[cell_block(0, b, c, 0)] = jnp.zeros_like(value)
+
+    def sum_copy(peer):
+        return to_device(
+            sum_send.at[peer], sum_recv.at[mine], sum_send_sem.at[peer], sum_recv_sem.at[mine], "dp", peer
+        )
+
+    def all_copy(peer):
+        return to_device(
+            all_send, all_recv.at[mine], all_send_sem.at[peer], all_recv_sem.at[mine], "dp", peer
+        )
+
+    def columns(owner):
+        return pl.ds(pl.multiple_of(owner * quarter, quarter), quarter)
+
+    for k in range(1, m):
+        peer = (mine + k) % m
+        sum_send[peer] = contract_last(out_taps[...], cot[columns(peer), :]).astype(sum_send.dtype)
+        sum_copy(peer).start()
+    own = contract_last(out_taps[...], cot[columns(mine), :])
     for k in range(1, m):
         source = (mine + k) % m
         to_device(
             sum_send.at[source], sum_recv.at[source], sum_send_sem.at[source], sum_recv_sem.at[source], "dp", source
         ).wait_recv()
         own = own + sum_recv[source].astype(jnp.float32)
-    grad[:, own_cut] = own
     all_send[...] = own.astype(all_send.dtype)
     for k in range(1, m):
         all_copy((mine + k) % m).start()
-
-    back_recv[me] = back_send[me]
+    grad[:, columns(mine)] = own
+
     for k in range(1, n):
         source = (me + k) % n
         to_device(
             back_send.at[source], back_recv.at[source], back_send_sem.at[source], back_recv_sem.at[source], "space", source
         ).wait_recv()
-    back_out[...] = back_recv[...]
+    for g in range(n):
+        cut = slice(g * group, (g + 1) * group)
+        pre_grad[cut, :] = (back_recv[g].astype(jnp.float32) * slope_of(pre[cut, :])).astype(pre_grad.dtype)
     for k in range(1, m):
         source = (mine + k) % m
         to_device(
             all_send, all_recv.at[source], all_send_sem.at[source], all_recv_sem.at[source], "dp", source
         ).wait_recv()
-        cut = pl.ds(pl.multiple_of(source * quarter, quarter), quarter)
-        grad[:, cut] = all_recv[source].astype(jnp.float32)
+        grad[:, columns(source)] = all_recv[source].astype(jnp.float32)
+
+    finish = lambda copy: copy.wait_send()
+    cot_copy(me, 2).wait_send()
+    for h in range(chips - 1):
+        cot_send(h, finish)
+        cot_pass(h + 1, False, finish)
+
+    @pl.when(me < n - 1)
+    def _():
+        for c in range(chunks):
+            rim_copy(c).wait_send()
+
     for k in range(1, n):
+        hid_copy((me + k) % n).wait_send()
         back_copy((me + k) % n).wait_send()
     for k in range(1, m):
         sum_copy((mine + k) % m).wait_send()
         all_copy((mine + k) % m).wait_send()
-
-
-def in_vmem(count):
-    return [pl.BlockSpec(memory_space=pltpu.VMEM)] * count
 
 
 def per_device(volume, w_first, w_second, cotangent):
@@ -413,71 +471,71 @@
     if volume.shape[2] != 2 or group % 16 or (last // m) % 128 or n % 2:
         return plain_device(volume, w_first, w_second, cotangent)
     planes = jnp.transpose(volume[0], (1, 2, 0, 3))
-    w_flat = w_first.reshape(27 * channels, out_channels)
     span = 4 * cells
     chunks = 2
-    pre, hidden = pl.pallas_call(
-        functools.partial(first_kernel, n, row_len, chunks),
+    rows = 27 * group
+    cot_planes = cotangent.shape[2]
+    out_cells = cot_planes * cells
+    quarter = last // m
+    bf16, f32 = jnp.bfloat16, jnp.float32
+    vmem = pl.BlockSpec(memory_space=pltpu.VMEM)
+    anywhere = pl.BlockSpec(memory_space=pl.ANY)
+    dma = pltpu.SemaphoreType.DMA
+    grad, pre_grad = pl.pallas_call(
+        functools.partial(section_kernel, n, m, row_len, chunks),
         out_shape=(
-            jax.ShapeDtypeStruct((out_channels, span), jnp.float32),
-            jax.ShapeDtypeStruct((n, group, span), jnp.bfloat16),
+            jax.ShapeDtypeStruct((rows, last), f32),
+            jax.ShapeDtypeStruct((out_channels, span), bf16),
         ),
-        in_specs=in_vmem(2),
-        out_specs=tuple(in_vmem(2)),
+        in_specs=[vmem, anywhere, anywhere, vmem],
+        out_specs=(vmem, vmem),
         scratch_shapes=[
-            pltpu.VMEM((9 * channels, span), jnp.bfloat16),
-            pltpu.VMEM((out_channels, span), jnp.bfloat16),
-            pltpu.VMEM((out_channels, span), jnp.bfloat16),
-            pltpu.VMEM((n, group, span), jnp.bfloat16),
-            pltpu.VMEM((n, group, span), jnp.bfloat16),
-            pltpu.SemaphoreType.DMA((chunks,)),
-            pltpu.SemaphoreType.DMA((chunks,)),
-            pltpu.SemaphoreType.DMA((n,)),
-            pltpu.SemaphoreType.DMA((n,)),
+            pltpu.VMEM((27 * channels, out_channels), bf16),
+            pltpu.VMEM((rows, last), bf16),
+            pltpu.VMEM((last, out_cells), bf16),
+            pltpu.VMEM((9 * channels, span), bf16),
+            pltpu.VMEM((out_channels, span), f32),
+            pltpu.VMEM((out_channels, span), bf16),
+            pltpu.VMEM((out_channels, span), bf16),
+            pltpu.VMEM((n, group, span), bf16),
+            pltpu.VMEM((n, group, span), bf16),
+            pltpu.VMEM((rows, out_cells), bf16),
+            pltpu.VMEM((rows, out_cells), f32),
+            pltpu.VMEM((n, group, span), bf16),
+            pltpu.VMEM((n, group, span), bf16),
+            pltpu.VMEM((m, rows, quarter), bf16),
+            pltpu.VMEM((m, rows, quarter), bf16),
+            pltpu.VMEM((rows, quarter), bf16),
+            pltpu.VMEM((m, rows, quarter), bf16),
+            dma((3,)),
+            dma((1,)),
+            dma((3, n)),
+            dma((n,)),
+            dma((chunks,)),
+            dma((chunks,)),
+            dma((n,)),
+            dma((n,)),
+            dma((n,)),
+            dma((n,)),
+            dma((m,)),
+            dma((m,)),
+            dma((m,)),
+            dma((m,)),
         ],
         compiler_params=pltpu.CompilerParams(
-            collective_id=0, has_side_effects=True, vmem_limit_bytes=40 * 2**20
+            collective_id=0, has_side_effects=True, vmem_limit_bytes=50 * 2**20
         ),
         cost_estimate=pl.CostEstimate(
-            flops=2 * 27 * channels * out_channels * span, bytes_accessed=6 * 2**20, transcendentals=0
+            flops=2 * 27 * channels * out_channels * span + 4 * rows * last * out_cells,
+            bytes_accessed=10 * 2**20,
+            transcendentals=0,
         ),
-    )(planes, w_flat)
-    cot = lax.all_gather(cotangent[0].reshape(cotangent.shape[1], -1), "space", axis=0, tiled=True)
-    rows = 27 * group
-    out_cells = cot.shape[1]
-    grad, back = pl.pallas_call(
-        functools.partial(second_kernel, n, m, row_len),
-        out_shape=(
-            jax.ShapeDtypeStruct((rows, last), jnp.float32),
-            jax.ShapeDtypeStruct((n, group, span), jnp.bfloat16),
-        ),
-        in_specs=in_vmem(3),
-        out_specs=tuple(in_vmem(2)),
-        scratch_shapes=[
-            pltpu.VMEM((rows, out_cells), jnp.bfloat16),
-            pltpu.VMEM((rows, out_cells), jnp.float32),
-            pltpu.VMEM((n, group, span), jnp.bfloat16),
-            pltpu.VMEM((n, group, span), jnp.bfloat16),
-            pltpu.VMEM((m, rows, last // m), jnp.bfloat16),
-            pltpu.VMEM((m, rows, last // m), jnp.bfloat16),
-            pltpu.VMEM((rows, last // m), jnp.bfloat16),
-            pltpu.VMEM((m, rows, last // m), jnp.bfloat16),
-            pltpu.SemaphoreType.DMA((n,)),
-            pltpu.SemaphoreType.DMA((n,)),
-            pltpu.SemaphoreType.DMA((m,)),
-            pltpu.SemaphoreType.DMA((m,)),
-            pltpu.SemaphoreType.DMA((m,)),
-            pltpu.SemaphoreType.DMA((m,)),
-        ],
-        compiler_params=pltpu.CompilerParams(
-            collective_id=1, has_side_effects=True, vmem_limit_bytes=40 * 2**20
-        ),
-        cost_estimate=pl.CostEstimate(
-            flops=4 * rows * last * out_cells, bytes_accessed=6 * 2**20, transcendentals=0
-        ),
-    )(hidden, w_second.reshape(rows, last), cot)
-    hidden_grad = back.reshape(out_channels, span)
-    pre_grad = (hidden_grad.astype(jnp.float32) * slope_of(pre)).astype(jnp.bfloat16)
+    )(
+        planes,
+        w_first.reshape(27 * channels, out_channels),
+        w_second.reshape(rows, last),
+        cotangent[0],
+    )
     return (
         grad.reshape(3, 3, 3, group, last),
         pre_grad.reshape(1, out_channels, 1, 4, cells),

time: 85.8 us -> 68.7 us (0.80)
  between operations: 14.1 us -> 0.66 us
  local copies, waits for them, and re-layouts: 9.24 us -> 6.57 us
    unnamed x9 -> x6, local copies, waits for them, and re-layouts: 8.07 us -> 5.4 us
    pallas_call x2 -> x1, Pallas kernels: 61.7 us -> 61.3 us  [per_device(): pl.pallas_call(functools.partial(section_kernel, n, m, row_len, chunks),...]
  transfers between devices with their start and end apart: 1 -> 0, of which waited for: 0 -> 0; matrix products, arithmetic and copies ran while one was open for 3% -> 0% of each run, Pallas kernels for 34% -> 0%
where the time goes in v2:
time: 68.7 us; the launch traced here: 68.5 us
  Pallas kernels  61.3 us (89%)
  local copies, waits for them, and re-layouts  6.57 us (10%)
    pallas_call x1, Pallas kernels, per_device(): pl.pallas_call(functools.partial(section_kernel, n, m, row_len, chunks),...  61.3 us
    unnamed x6, local copies, waits for them, and re-layouts  5.4 us

profile of v2, /device:TPU:0, one launch (start us, length us, event | category | flops | bytes accessed | tf_op | source)
XLA Modules:
  0.0 68.5 jit_solution(6617503557606285008)
XLA Ops:
  0.6 0.0 copy-start
  0.6 0.0 copy-start.1
  0.6 4.2 %copy.9 = bf16[1,128,2,16,256]{4,1,3,2,0:T(8,128)(2,1)} copy(bf16[1,128,2,16,256]{4,3,2,1,0:T(8,128)(2,1)} %param.4) | data formatting | bytes 4194304 | tf_op args[0]
  4.8 0.0 copy-done
  4.8 0.0 copy-done.1
  4.8 61.3 %shard_map.59 = (f32[864,512]{1,0:T(8,128)S(1)}, bf16[256,1024]{1,0:T(8,128)(2,1)S(1)}) custom-call(bf16[2,16,128,256]{3,2,1,0:T(8,128)(2,1)} %bitcast.13, bf16[3456,256]{1,0:T(8,128)(2,1)} %bitcast.15, bf16[864,512]{1,0:T(8,128)(2,1)S(1)} %bitcast.11, bf16[64,4,256]{2,1,0:T(4,128)(2,1)S(1)} %bitcast.12), custom_call_target="tpu_custom_call" | custom-call | flops 3623878656 | bytes 10485760 | tf_op jit(solution)/shard_map/pallas_call | solution.py:484
  66.1 1.2 %reshape.19 = bf16[1,256,1,4,256]{4,3,1,2,0:T(4,128)(2,1)} reshape(bf16[256,1024]{1,0:T(8,128)(2,1)S(1)} %get-tuple-element.5) | data formatting | bytes 1048576 | tf_op jit(solution)/shard_map/reshape | solution.py:541
  67.3 1.2 %copy.11 = f32[3,3,3,32,512]{4,3,2,1,0:T(8,128)} copy(f32[3,3,3,32,512]{4,3,2,1,0:T(8,128)S(1)} %bitcast.10) | data formatting | bytes 3538944
Async XLA Ops:
  0.6 4.2 %copy-start = (bf16[3,3,3,32,512]{4,3,2,1,0:T(8,128)(2,1)S(1)}, bf16[3,3,3,32,512]{4,3,2,1,0:T(8,128)(2,1)}, u32[]{:S(2)}) copy-start(bf16[3,3,3,32,512]{4,3,2,1,0:T(8,128)(2,1)} %param.6) | copy-start | bytes 2654212
  0.6 4.2 %copy-start.1 = (bf16[1,64,4,256]{3,2,1,0:T(4,128)(2,1)S(1)}, bf16[1,64,4,256]{3,2,1,0:T(4,128)(2,1)}, u32[]{:S(2)}) copy-start(bf16[1,64,4,256]{3,2,1,0:T(4,128)(2,1)} %param.7) | copy-start | bytes 393220

commit v3 on v2

--- a/solution.py
+++ b/solution.py
@@ -183,15 +183,16 @@
 
 def greet(axes):
     barrier = pltpu.get_barrier_semaphore()
-    total = 0
     for axis, size in axes:
         me = lax.axis_index(axis)
         for k in range(1, size):
             pl.semaphore_signal(
                 barrier, inc=1, device_id={axis: (me + k) % size}, device_id_type=pl.DeviceIdType.MESH
             )
-        total += size - 1
-    pl.semaphore_wait(barrier, total)
+
+
+def await_greetings(axes):
+    pl.semaphore_wait(pltpu.get_barrier_semaphore(), sum(size - 1 for _, size in axes))
 
 
 def to_device(src, dst, send_sem, recv_sem, axis, peer):
@@ -224,7 +225,8 @@
     out_channels = w1.shape[1]
     wide = out_channels // chunks
     group = out_channels // n
-    per_chunk = n // chunks
+    half = group // chunks
+    tap_rows = 27 * half
     depth = n
     planes = depth // 2
     quarter = cot.shape[0] // m
@@ -234,6 +236,8 @@
         cut = pl.ds(a * rows, rows)
         return pltpu.make_async_copy(w1_hbm.at[cut], w1.at[cut], w1_sem.at[a])
 
+    axes = [("space", n), ("dp", m)]
+    greet(axes)
     for a in (0, 2, 1):
         w1_copy(a).start()
     w2_copy = pltpu.make_async_copy(w2_hbm, w2, w2_sem.at[0])
@@ -241,7 +245,8 @@
     own_rows = pl.ds(pl.multiple_of(me * share, share), share)
     for s in range(planes):
         cot[own_rows, s * cells : (s + 1) * cells] = cot_own[:, s, :]
-    greet([("space", n), ("dp", m)])
+    fill_taps(vol.at[1], taps, row_len)
+    await_greetings(axes)
 
     def cot_copy(block, way):
         cut = pl.ds(pl.multiple_of(block * share, share), share)
@@ -282,7 +287,6 @@
     cot_copy(me, 2).start()
     cot_send(0, start)
 
-    fill_taps(vol.at[1], taps, row_len)
     w1_copy(0).wait()
 
     def rim_copy(c):
@@ -291,9 +295,12 @@
             part.at[cut], rim.at[cut], rim_send_sem.at[c], rim_recv_sem.at[c], "space", (me + 1) % n
         )
 
+    before = contract_first(w1[0:rows, :], taps[...])
     for c in range(chunks):
-        cut = slice(c * wide, (c + 1) * wide)
-        part[cut, :] = contract_first(w1[0:rows, cut], taps[...]).astype(part.dtype)
+        for g in range(n):
+            from_row = g * group + c * half
+            to_row = c * wide + g * half
+            part[to_row : to_row + half, :] = before[from_row : from_row + half].astype(part.dtype)
 
         @pl.when(me < n - 1)
         def _():
@@ -308,40 +315,106 @@
     cot_pass(1, True, start)
     cot_send(1, start)
 
-    def hid_copy(peer):
+    def hid_copy(c, peer):
         return to_device(
-            hid_send.at[peer], hid_recv.at[me], hid_send_sem.at[peer], hid_recv_sem.at[me], "space", peer
+            hid_send.at[c, peer], hid_recv.at[c, me], hid_send_sem.at[c, peer], hid_recv_sem.at[c, me], "space", peer
         )
 
     for c in range(chunks):
-        cut = slice(c * wide, (c + 1) * wide)
 
         @pl.when(me > 0)
         def _():
             rim_copy(c).wait_recv()
-            pre[cut, :] += rim[cut, :].astype(jnp.float32)
-
-        for g in range(per_chunk):
-            at = c * per_chunk + g
-            hid_send[at] = activate(pre[at * group : (at + 1) * group, :]).astype(hid_send.dtype)
-        for k in range(per_chunk):
-            peer = c * per_chunk + (me + k + 1) % per_chunk
-
-            @pl.when(peer != me)
-            def _():
-                hid_copy(peer).start()
+            for g in range(n):
+                to_row = g * group + c * half
+                from_row = c * wide + g * half
+                pre[to_row : to_row + half, :] += rim[from_row : from_row + half, :].astype(jnp.float32)
+
+        for g in range(n):
+            at = g * group + c * half
+            hid_send[c, g] = activate(pre[at : at + half, :]).astype(hid_send.dtype)
+        for k in range(1, n):
+            hid_copy(c, (me + k) % n).start()
 
     for h in range(2, chips):
         cot_pass(h, True, start)
         if h + 1 < chips:
             cot_send(h, start)
-    hid_recv[me] = hid_send[me]
+    for c in range(chunks):
+        hid_recv[c, me] = hid_send[c, me]
     for z in range(chips):
         cot_copy(2 * z + 1 - core, 2).wait_recv()
 
     def cell_block(a, b, c, s):
         top = ((a * 3 + b) * 3 + c) * group
         return (slice(top, top + group), slice(s * cells, (s + 1) * cells))
+
+    def sum_copy(c, peer):
+        return to_device(
+            sum_send.at[c, peer], sum_recv.at[c, mine], sum_send_sem.at[c, peer], sum_recv_sem.at[c, mine], "dp", peer
+        )
+
+    def all_copy(c, peer):
+        return to_device(
+            all_send.at[c], all_recv.at[c, mine], all_send_sem.at[c, peer], all_recv_sem.at[c, mine], "dp", peer
+        )
+
+    def columns(owner):
+        return pl.ds(pl.multiple_of(owner * quarter, quarter), quarter)
+
+    def await_hidden(c):
+        for k in range(1, n):
+            source = (me + k) % n
+            to_device(
+                hid_send.at[c, source], hid_recv.at[c, source],
+                hid_send_sem.at[c, source], hid_recv_sem.at[c, source], "space", source,
+            ).wait_recv()
+
+    def weight_part(c):
+        def tap_block(a, b, e, s):
+            top = c * tap_rows + ((a * 3 + b) * 3 + e) * half
+            return (slice(top, top + half), slice(s * cells, (s + 1) * cells))
+
+        for x in range(depth):
+            for b in range(3):
+                for e in range(3):
+                    phase = 2 * ((b + 1) % 2) + (e + 1) % 2
+                    value = moved_cells(
+                        hid_recv[c, x, :, phase * cells : (phase + 1) * cells], b == 0, e == 0, row_len
+                    )
+                    if x % 2 == 0:
+                        out_taps[tap_block(1, b, e, x // 2)] = value
+                    else:
+                        out_taps[tap_block(2, b, e, x // 2)] = value
+                        if x // 2 + 1 < planes:
+                            out_taps[tap_block(0, b, e, x // 2 + 1)] = value
+                    if x == 0:
+                        out_taps[tap_block(0, b, e, 0)] = jnp.zeros_like(value)
+        mine_taps = slice(c * tap_rows, (c + 1) * tap_rows)
+        for k in range(1, m):
+            peer = (mine + k) % m
+            sum_send[c, peer] = contract_last(out_taps[mine_taps, :], cot[columns(peer), :]).astype(sum_send.dtype)
+            sum_copy(c, peer).start()
+        own = contract_last(out_taps[mine_taps, :], cot[columns(mine), :])
+        grad[:, c * half : (c + 1) * half, columns(mine)] = own.reshape(27, half, quarter)
+
+    def sum_part(c):
+        at = slice(c * half, (c + 1) * half)
+        own = grad[:, at, columns(mine)].reshape(tap_rows, quarter)
+        for k in range(1, m):
+            source = (mine + k) % m
+            to_device(
+                sum_send.at[c, source], sum_recv.at[c, source],
+                sum_send_sem.at[c, source], sum_recv_sem.at[c, source], "dp", source,
+            ).wait_recv()
+            own = own + sum_recv[c, source].astype(jnp.float32)
+        all_send[c] = own.astype(all_send.dtype)
+        for k in range(1, m):
+            all_copy(c, (mine + k) % m).start()
+        grad[:, at, columns(mine)] = own.reshape(27, half, quarter)
+
+    await_hidden(0)
+    weight_part(0)
 
     w2_copy.wait()
     terms[...] = jnp.dot(w2[...], cot[...], preferred_element_type=jnp.float32)
@@ -371,59 +444,15 @@
         ]
         for phase in range(4):
             back_send[x, :, phase * cells : (phase + 1) * cells] = phases[phase].astype(back_send.dtype)
-    for k in range(1, n):
-        back_copy((me + k) % n).start()
+    for c in range(1, chunks):
+        await_hidden(c)
+        if c == chunks - 1:
+            for k in range(1, n):
+                back_copy((me + k) % n).start()
+        weight_part(c)
+        sum_part(c - 1)
     back_recv[me] = back_send[me]
-
-    for k in range(1, n):
-        source = (me + k) % n
-        to_device(
-            hid_send.at[source], hid_recv.at[source], hid_send_sem.at[source], hid_recv_sem.at[source], "space", source
-        ).wait_recv()
-    for x in range(depth):
-        for b in range(3):
-            for c in range(3):
-                phase = 2 * ((b + 1) % 2) + (c + 1) % 2
-                value = moved_cells(
-                    hid_recv[x, :, phase * cells : (phase + 1) * cells], b == 0, c == 0, row_len
-                )
-                if x % 2 == 0:
-                    out_taps[cell_block(1, b, c, x // 2)] = value
-                else:
-                    out_taps[cell_block(2, b, c, x // 2)] = value
-                    if x // 2 + 1 < planes:
-                        out_taps[cell_block(0, b, c, x // 2 + 1)] = value
-                if x == 0:
-                    out_taps[cell_block(0, b, c, 0)] = jnp.zeros_like(value)
-
-    def sum_copy(peer):
-        return to_device(
-            sum_send.at[peer], sum_recv.at[mine], sum_send_sem.at[peer], sum_recv_sem.at[mine], "dp", peer
-        )
-
-    def all_copy(peer):
-        return to_device(
-            all_send, all_recv.at[mine], all_send_sem.at[peer], all_recv_sem.at[mine], "dp", peer
-        )
-
-    def columns(owner):
-        return pl.ds(pl.multiple_of(owner * quarter, quarter), quarter)
-
-    for k in range(1, m):
-        peer = (mine + k) % m
-        sum_send[peer] = contract_last(out_taps[...], cot[columns(peer), :]).astype(sum_send.dtype)
-        sum_copy(peer).start()
-    own = contract_last(out_taps[...], cot[columns(mine), :])
-    for k in range(1, m):
-        source = (mine + k) % m
-        to_device(
-            sum_send.at[source], sum_recv.at[source], sum_send_sem.at[source], sum_recv_sem.at[source], "dp", source
-        ).wait_recv()
-        own = own + sum_recv[source].astype(jnp.float32)
-    all_send[...] = own.astype(all_send.dtype)
-    for k in range(1, m):
-        all_copy((mine + k) % m).start()
-    grad[:, columns(mine)] = own
+    sum_part(chunks - 1)
 
     for k in range(1, n):
         source = (me + k) % n
@@ -433,12 +462,16 @@
     for g in range(n):
         cut = slice(g * group, (g + 1) * group)
         pre_grad[cut, :] = (back_recv[g].astype(jnp.float32) * slope_of(pre[cut, :])).astype(pre_grad.dtype)
-    for k in range(1, m):
-        source = (mine + k) % m
-        to_device(
-            all_send, all_recv.at[source], all_send_sem.at[source], all_recv_sem.at[source], "dp", source
-        ).wait_recv()
-        grad[:, columns(source)] = all_recv[source].astype(jnp.float32)
+    for c in range(chunks):
+        for k in range(1, m):
+            source = (mine + k) % m
+            to_device(
+                all_send.at[c], all_recv.at[c, source],
+                all_send_sem.at[c, source], all_recv_sem.at[c, source], "dp", source,
+            ).wait_recv()
+            grad[:, c * half : (c + 1) * half, columns(source)] = (
+                all_recv[c, source].astype(jnp.float32).reshape(27, half, quarter)
+            )
 
     finish = lambda copy: copy.wait_send()
     cot_copy(me, 2).wait_send()
@@ -452,11 +485,13 @@
             rim_copy(c).wait_send()
 
     for k in range(1, n):
-        hid_copy((me + k) % n).wait_send()
         back_copy((me + k) % n).wait_send()
-    for k in range(1, m):
-        sum_copy((mine + k) % m).wait_send()
-        all_copy((mine + k) % m).wait_send()
+    for c in range(chunks):
+        for k in range(1, n):
+            hid_copy(c, (me + k) % n).wait_send()
+        for k in range(1, m):
+            sum_copy(c, (mine + k) % m).wait_send()
+            all_copy(c, (mine + k) % m).wait_send()
 
 
 def per_device(volume, w_first, w_second, cotangent):
@@ -468,7 +503,7 @@
     group = w_second.shape[3]
     last = w_second.shape[4]
     row_len = WID // 4
-    if volume.shape[2] != 2 or group % 16 or (last // m) % 128 or n % 2:
+    if volume.shape[2] != 2 or group % 32 or (last // m) % 128 or n % 2:
         return plain_device(volume, w_first, w_second, cotangent)
     planes = jnp.transpose(volume[0], (1, 2, 0, 3))
     span = 4 * cells
@@ -484,7 +519,7 @@
     grad, pre_grad = pl.pallas_call(
         functools.partial(section_kernel, n, m, row_len, chunks),
         out_shape=(
-            jax.ShapeDtypeStruct((rows, last), f32),
+            jax.ShapeDtypeStruct((27, group, last), f32),
             jax.ShapeDtypeStruct((out_channels, span), bf16),
         ),
         in_specs=[vmem, anywhere, anywhere, vmem],
@@ -497,30 +532,30 @@
             pltpu.VMEM((out_channels, span), f32),
             pltpu.VMEM((out_channels, span), bf16),
             pltpu.VMEM((out_channels, span), bf16),
-            pltpu.VMEM((n, group, span), bf16),
-            pltpu.VMEM((n, group, span), bf16),
+            pltpu.VMEM((chunks, n, group // chunks, span), bf16),
+            pltpu.VMEM((chunks, n, group // chunks, span), bf16),
             pltpu.VMEM((rows, out_cells), bf16),
             pltpu.VMEM((rows, out_cells), f32),
             pltpu.VMEM((n, group, span), bf16),
             pltpu.VMEM((n, group, span), bf16),
-            pltpu.VMEM((m, rows, quarter), bf16),
-            pltpu.VMEM((m, rows, quarter), bf16),
-            pltpu.VMEM((rows, quarter), bf16),
-            pltpu.VMEM((m, rows, quarter), bf16),
+            pltpu.VMEM((chunks, m, rows // chunks, quarter), bf16),
+            pltpu.VMEM((chunks, m, rows // chunks, quarter), bf16),
+            pltpu.VMEM((chunks, rows // chunks, quarter), bf16),
+            pltpu.VMEM((chunks, m, rows // chunks, quarter), bf16),
             dma((3,)),
             dma((1,)),
             dma((3, n)),
             dma((n,)),
             dma((chunks,)),
             dma((chunks,)),
+            dma((chunks, n)),
+            dma((chunks, n)),
             dma((n,)),
             dma((n,)),
-            dma((n,)),
-            dma((n,)),
-            dma((m,)),
-            dma((m,)),
-            dma((m,)),
-            dma((m,)),
+            dma((chunks, m)),
+            dma((chunks, m)),
+            dma((chunks, m)),
+            dma((chunks, m)),
         ],
         compiler_params=pltpu.CompilerParams(
             collective_id=0, has_side_effects=True, vmem_limit_bytes=50 * 2**20

time: 68.7 us -> 59.2 us (0.86)
  Pallas kernels: 61.3 us -> 51.4 us
    pallas_call x1, Pallas kernels: 61.3 us -> 51.4 us  [per_device(): pl.pallas_call(functools.partial(section_kernel, n, m, row_len, chunks),...]
where the time goes in v3:
time: 59.2 us; the launch traced here: 58.7 us
  Pallas kernels  51.4 us (87%)
  local copies, waits for them, and re-layouts  6.57 us (11%)
  between operations  0.66 us (1%)
    pallas_call x1, Pallas kernels, per_device(): pl.pallas_call(functools.partial(section_kernel, n, m, row_len, chunks),...  51.4 us
    unnamed x6, local copies, waits for them, and re-layouts  5.4 us

profile of v3, /device:TPU:0, one launch (start us, length us, event | category | flops | bytes accessed | tf_op | source)
XLA Modules:
  0.0 58.7 jit_solution(13659254184457667970)
XLA Ops:
  0.6 0.0 copy-start
  0.6 0.0 copy-start.1
  0.6 4.2 %copy.9 = bf16[1,128,2,16,256]{4,1,3,2,0:T(8,128)(2,1)} copy(bf16[1,128,2,16,256]{4,3,2,1,0:T(8,128)(2,1)} %param.4) | data formatting | bytes 4194304 | tf_op args[0]
  4.8 0.0 copy-done
  4.8 0.0 copy-done.1
  4.8 51.4 %shard_map.59 = (f32[27,32,512]{2,1,0:T(8,128)S(1)}, bf16[256,1024]{1,0:T(8,128)(2,1)S(1)}) custom-call(bf16[2,16,128,256]{3,2,1,0:T(8,128)(2,1)} %bitcast.13, bf16[3456,256]{1,0:T(8,128)(2,1)} %bitcast.15, bf16[864,512]{1,0:T(8,128)(2,1)S(1)} %bitcast.11, bf16[64,4,256]{2,1,0:T(4,128)(2,1)S(1)} %bitcast.12), custom_call_target="tpu_custom_call" | custom-call | flops 3623878656 | bytes 10485760 | tf_op jit(solution)/shard_map/pallas_call | solution.py:519
  56.3 1.2 %reshape.19 = bf16[1,256,1,4,256]{4,3,1,2,0:T(4,128)(2,1)} reshape(bf16[256,1024]{1,0:T(8,128)(2,1)S(1)} %get-tuple-element.5) | data formatting | bytes 1048576 | tf_op jit(solution)/shard_map/reshape | solution.py:576
  57.4 1.2 %copy.11 = f32[3,3,3,32,512]{4,3,2,1,0:T(8,128)} copy(f32[3,3,3,32,512]{4,3,2,1,0:T(8,128)S(1)} %bitcast.10) | data formatting | bytes 3538944
Async XLA Ops:
  0.6 4.2 %copy-start = (bf16[3,3,3,32,512]{4,3,2,1,0:T(8,128)(2,1)S(1)}, bf16[3,3,3,32,512]{4,3,2,1,0:T(8,128)(2,1)}, u32[]{:S(2)}) copy-start(bf16[3,3,3,32,512]{4,3,2,1,0:T(8,128)(2,1)} %param.6) | copy-start | bytes 2654212
  0.6 4.2 %copy-start.1 = (bf16[1,64,4,256]{3,2,1,0:T(4,128)(2,1)S(1)}, bf16[1,64,4,256]{3,2,1,0:T(4,128)(2,1)}, u32[]{:S(2)}) copy-start(bf16[1,64,4,256]{3,2,1,0:T(4,128)(2,1)} %param.7) | copy-start | bytes 393220

commit v4 on v3

--- a/solution.py
+++ b/solution.py
@@ -558,7 +558,7 @@
             dma((chunks, m)),
         ],
         compiler_params=pltpu.CompilerParams(
-            collective_id=0, has_side_effects=True, vmem_limit_bytes=50 * 2**20
+            collective_id=0, has_side_effects=True, vmem_limit_bytes=32 * 2**20
         ),
         cost_estimate=pl.CostEstimate(
             flops=2 * 27 * channels * out_channels * span + 4 * rows * last * out_cells,

time: 59.2 us -> 56.4 us (0.953)
  Pallas kernels: 51.4 us -> 49.9 us
  local copies, waits for them, and re-layouts: 6.57 us -> 5.3 us
    pallas_call x1, Pallas kernels: 51.4 us -> 49.9 us  [per_device(): pl.pallas_call(functools.partial(section_kernel, n, m, row_len, chunks),...]
    unnamed x6 -> x8, local copies, waits for them, and re-layouts: 5.4 us -> 4.13 us
where the time goes in v4:
time: 56.4 us; the launch traced here: 55.9 us
  Pallas kernels  49.9 us (88%)
  local copies, waits for them, and re-layouts  5.3 us (9%)
  between operations  0.69 us (1%)
    pallas_call x1, Pallas kernels, per_device(): pl.pallas_call(functools.partial(section_kernel, n, m, row_len, chunks),...  49.9 us
    unnamed x8, local copies, waits for them, and re-layouts  4.13 us
    reshape x1, local copies, waits for them, and re-layouts, per_device(): pre_grad.reshape(1, out_channels, 1, 4, cells)  1.17 us

profile of v4, /device:TPU:0, one launch (start us, length us, event | category | flops | bytes accessed | tf_op | source)
XLA Modules:
  0.0 55.9 jit_solution(17990097095862838880)
XLA Ops:
  0.6 0.0 copy-start
  0.6 0.0 copy-start.1
  0.7 0.0 copy-start.2
  0.7 2.9 %copy.9 = bf16[1,128,2,16,256]{4,1,3,2,0:T(8,128)(2,1)S(1)} copy(bf16[1,128,2,16,256]{4,3,2,1,0:T(8,128)(2,1)} %param.4) | data formatting | bytes 4194304 | tf_op args[0]
  3.6 0.0 copy-done
  3.6 0.0 copy-done.1
  3.6 0.0 copy-done.2
  3.6 49.9 %shard_map.59 = (f32[27,32,512]{2,1,0:T(8,128)S(1)}, bf16[256,1024]{1,0:T(8,128)(2,1)S(1)}) custom-call(bf16[2,16,128,256]{3,2,1,0:T(8,128)(2,1)S(1)} %bitcast.10, bf16[3456,256]{1,0:T(8,128)(2,1)S(1)} %bitcast.12, bf16[864,512]{1,0:T(8,128)(2,1)S(1)} %bitcast.13, bf16[64,4,256]{2,1,0:T(4,128)(2,1)S(1)} %bitcast.14), custom_call_target="tpu_custom_call" | custom-call | flops 3623878656 | bytes 10485760 | tf_op jit(solution)/shard_map/pallas_call | solution.py:519
  53.5 1.2 %reshape.19 = bf16[1,256,1,4,256]{4,3,1,2,0:T(4,128)(2,1)} reshape(bf16[256,1024]{1,0:T(8,128)(2,1)S(1)} %get-tuple-element.5) | data formatting | bytes 1048576 | tf_op jit(solution)/shard_map/reshape | solution.py:576
  54.7 1.2 %copy.11 = f32[3,3,3,32,512]{4,3,2,1,0:T(8,128)} copy(f32[3,3,3,32,512]{4,3,2,1,0:T(8,128)S(1)} %bitcast.11) | data formatting | bytes 3538944
Async XLA Ops:
  0.6 3.0 %copy-start = (bf16[3,3,3,128,256]{4,3,2,1,0:T(8,128)(2,1)S(1)}, bf16[3,3,3,128,256]{4,3,2,1,0:T(8,128)(2,1)}, u32[]{:S(2)}) copy-start(bf16[3,3,3,128,256]{4,3,2,1,0:T(8,128)(2,1)} %param.5) | copy-start | bytes 5308420
  0.6 3.0 %copy-start.1 = (bf16[3,3,3,32,512]{4,3,2,1,0:T(8,128)(2,1)S(1)}, bf16[3,3,3,32,512]{4,3,2,1,0:T(8,128)(2,1)}, u32[]{:S(2)}) copy-start(bf16[3,3,3,32,512]{4,3,2,1,0:T(8,128)(2,1)} %param.6) | copy-start | bytes 2654212
  0.7 3.0 %copy-start.2 = (bf16[1,64,4,256]{3,2,1,0:T(4,128)(2,1)S(1)}, bf16[1,64,4,256]{3,2,1,0:T(4,128)(2,1)}, u32[]{:S(2)}) copy-start(bf16[1,64,4,256]{3,2,1,0:T(4,128)(2,1)} %param.7) | copy-start | bytes 393220
